TPU v7x, 32 devices: a whole 2x2x4 slice. The times are simulated.
32 devices in a mesh: head: 4 (over z), key: 8 (over y, x, core).
Axes of the slice: x: 2, y: 2, z: 4, core: 2. Of those that a mesh axis runs over, the one named last changes fastest.
Arguments:
- q_latent: bfloat16 [128, 256, 576], P('head'), may hold values from -48 to 48
- k_latent: bfloat16 [8192, 576], P('key'), may hold values from -6 to 6
- q_index: bfloat16 [256, 8192], P('head'), may hold values from -8 to 8
- k_index: bfloat16 [8192, 128], P('key'), may hold values from -6 to 6
- head_weight: float32 [256, 64], P('head'), may hold values from -4 to 4, as said below
- loss_weight: float32 [256], P('head'), may hold values from 2048 to 16384
- query_pos: int32 [256], replicated, may hold values from 0 to 8191, as said below
- key_start: int32 [256], replicated, may hold values from 0 to 8191, as said below
Outputs:
- grad_query: float32 [256, 8192], P('head', 'key')
- grad_key: float32 [8192, 128], P('key')
- grad_weight: float32 [256, 64], P('head', 'key')
Inputs may be any that keep to these rules, and one draw needn't show every extreme that they name: `head_weight`: indexer head weights, of either sign. Query t sees the keys key_start[t] to query_pos[t]; some query sits at position 8191 and some at 0. key_start[t] <= query_pos[t] for every query t; some query starts at 0 and some at 8191.
All inputs are finite; a program needn't handle non-finite values.
Results may differ from a plain program's by a relative error of at most 0.0028.
Values sent between devices are 32-bit elements; how exact they have to be, the bound alone decides.
A program may use at most 128 MiB of HBM per device.

v0:
```python
import math

import jax
import jax.numpy as jnp
from jax import lax
from jax.sharding import PartitionSpec as P

H = 128
QK_DIM = 192


masked_low = -1e30


def joined(x, axis, combine):
    everything = jax.tree.map(lambda part: lax.all_gather(part, axis), x)
    first = jax.tree.map(lambda part: part[0], everything)

    def lap(k, so_far):
        return combine(so_far, jax.tree.map(lambda part: part[k], everything))

    return lax.fori_loop(1, lax.axis_size(axis), lap, first)


def local_stats(scores, seen_mask):
    masked = jnp.where(seen_mask, scores, masked_low)
    highest = jnp.max(masked, axis=-1)
    exponents = jnp.where(seen_mask, jnp.exp(scores - highest[..., None]), 0.0)
    return (highest, jnp.sum(exponents, axis=-1))


def combine_all(former, latter):
    merged = []
    for offset in range(0, len(former), 2):
        highest = jnp.maximum(former[offset], latter[offset])
        combined = former[offset + 1] * jnp.exp(former[offset] - highest) + latter[
            offset + 1
        ] * jnp.exp(latter[offset] - highest)
        merged.append(highest)
        merged.append(combined)
    return tuple(merged)


def shards(q_latent, k_latent, q_index, k_index, head_weight, loss_weight, query_pos, key_start):
    keys_here = k_latent.shape[0]
    rows_here, index_width = q_index.shape
    index_heads = head_weight.shape[1]
    index_dim = k_index.shape[1]
    score_scale = 1.0 / math.sqrt(QK_DIM)
    index_scale = 1.0 / math.sqrt(index_dim)
    positions = lax.axis_index("key") * keys_here + jnp.arange(keys_here, dtype=jnp.int32)
    visible = (positions[None, :] >= key_start[:, None]) & (
        positions[None, :] <= query_pos[:, None]
    )

    def main_scores(q_rows):
        return (
            jnp.einsum("qd,sd->qs", q_rows, k_latent, preferred_element_type=jnp.float32)
            * score_scale
        )

    main_high, main_sum = lax.map(
        lambda q_head: local_stats(main_scores(q_head), visible), q_latent
    )
    row_start = lax.axis_index("head") * rows_here
    own_pos = lax.dynamic_slice_in_dim(query_pos, row_start, rows_here)
    own_start = lax.dynamic_slice_in_dim(key_start, row_start, rows_here)
    own_visible = (positions[None, :] >= own_start[:, None]) & (
        positions[None, :] <= own_pos[:, None]
    )
    q_heads = q_index.reshape(rows_here, index_heads, index_dim)
    head_dots = jnp.einsum("qjd,sd->qjs", q_heads, k_index, preferred_element_type=jnp.float32)
    rectified = jnp.maximum(head_dots, 0.0)
    index_scores = jnp.sum(head_weight[:, :, None] * rectified, axis=1) * index_scale
    index_high, index_sum = local_stats(index_scores, own_visible)
    main_high, main_sum = joined((main_high, main_sum), "key", combine_all)
    index_high, index_sum = joined((index_high, index_sum), "key", combine_all)

    def add_head(running, entries):
        scores = main_scores(entries[0])
        probabilities = (
            jnp.where(visible, jnp.exp(scores - entries[1][:, None]), 0.0) / entries[2][:, None]
        )
        return (running + probabilities, None)

    start_value = jnp.zeros((q_latent.shape[1], keys_here), jnp.float32)
    summed, _ = lax.scan(add_head, start_value, (q_latent, main_high, main_sum))
    target = lax.psum_scatter(summed, "head", scatter_dimension=0, tiled=True)
    target = target / H
    index_probs = (
        jnp.where(own_visible, jnp.exp(index_scores - index_high[:, None]), 0.0)
        / index_sum[:, None]
    )
    grad_scores = jnp.where(own_visible, loss_weight[:, None] * (index_probs - target), 0.0)
    head_coef = head_weight * index_scale
    head_grad = jnp.where(
        head_dots > 0.0, grad_scores[:, None, :] * head_coef[:, :, None], 0.0
    ).astype(jnp.bfloat16)
    query_part = jnp.einsum(
        "qjs,sd->qjd", head_grad, k_index, preferred_element_type=jnp.float32
    ).reshape(rows_here, index_width)
    key_part = jnp.einsum("qjs,qjd->sd", head_grad, q_heads, preferred_element_type=jnp.float32)
    weight_part = jnp.sum(grad_scores[:, None, :] * rectified, axis=2)
    grad_query, grad_weight = (
        lax.psum_scatter(query_part, "key", scatter_dimension=1, tiled=True),
        lax.psum_scatter(weight_part, "key", scatter_dimension=1, tiled=True),
    )
    grad_key = lax.psum(key_part, "head")
    return (grad_query, grad_key, grad_weight * index_scale)


def solution(mesh):
    return jax.shard_map(
        shards,
        mesh=mesh,
        in_specs=(
            P("head", None, None),
            P("key", None),
            P("head", None),
            P("key", None),
            P("head", None),
            P("head"),
            P(),
            P(),
        ),
        out_specs=(P("head", "key"), P("key", None), P("head", "key")),
        check_vma=False,
    )
```

profile of v0, /device:TPU:0, one launch (start us, length us, event | category | flops | bytes accessed | tf_op | source)
XLA Modules:
  0.0 340.0 jit_solution(1961163912062530262)
XLA Ops:
  7.3 106.2 %while.60 = (s32[]{:T(128)}, f32[32,256]{1,0:T(8,128)S(1)}, f32[32,256]{1,0:T(8,128)S(1)}, bf16[32,256,576]{1,2,0:T(8,128)(2,1)}, bf16[1024,576]{0,1:T(8,128)(2,...) while((s32[]{:T(128)}, f32[32,256]{1,0:T(8,128)S(1)}, ...), condition=%wide.region_8.9_spmd.clone, body=%wide.region_5.8_spmd.clone.sunk | while | flops 305135104 | bytes 3591289 | solution.py:62
  10.6 2.1 select_reduce_fusion.6
  17.2 2.1 select_reduce_fusion.6
  20.6 2.1 select_reduce_fusion.6
  23.9 2.1 select_reduce_fusion.6
  30.5 2.1 select_reduce_fusion.6
  37.1 2.1 select_reduce_fusion.6
  43.8 2.1 select_reduce_fusion.6
  47.1 2.1 select_reduce_fusion.6
  50.4 2.1 select_reduce_fusion.6
  57.0 2.1 select_reduce_fusion.6
  60.4 2.1 select_reduce_fusion.6
  63.7 2.1 select_reduce_fusion.6
  70.3 2.1 select_reduce_fusion.6
  77.0 2.1 select_reduce_fusion.6
  83.6 2.1 select_reduce_fusion.6
  90.2 2.1 select_reduce_fusion.6
  96.9 2.1 select_reduce_fusion.6
  103.5 2.1 select_reduce_fusion.6
  110.1 2.1 select_reduce_fusion.6
  113.5 10.8 %all-gather.3 = f32[256,256]{1,0:T(8,128)S(1)} all-gather(f32[32,256]{1,0:T(8,128)S(1)} %get-tuple-element.342), channel_id=5, replica_groups=mesh['head'=4,'key'=8] {'key'}, dimensions={0}, use_global_device_ids=true | all-gather | bytes 294912 | tf_op jit(solution)/shard_map/all_gather | solution.py:16
  124.2 9.3 %all-gather.2 = f32[256,256]{1,0:T(8,128)S(1)} all-gather(f32[32,256]{1,0:T(8,128)S(1)} %get-tuple-element.341), channel_id=4, replica_groups=mesh['head'=4,'key'=8] {'key'}, dimensions={0}, use_global_device_ids=true | all-gather | bytes 294912 | tf_op jit(solution)/shard_map/all_gather | solution.py:16
  133.9 77.0 %while.61 = (s32[]{:T(128)}, f32[256,1024]{1,0:T(8,128)S(1)}, bf16[32,256,576]{1,2,0:T(8,128)(2,1)}, bf16[1024,576]{0,1:T(8,128)(2,1)}, f32[32,256]{1,0:T(8,128)...) while((s32[]{:T(128)}, f32[256,1024]{1,0:T(8,128)S(1)}, ...), condition=%wide.region_12.13_spmd.clone, body=%wide.region_11.12_spmd.clone.sunk | while | flops 304349184 | bytes 3584135 | solution.py:87
  134.0 2.4 fusion.41
  136.4 2.4 fusion.41
  138.8 2.4 fusion.41
  141.2 2.4 fusion.41
  143.6 2.4 fusion.41
  146.0 2.4 fusion.41
  148.5 2.4 fusion.41
  150.9 2.4 fusion.41
  153.3 2.4 fusion.41
  155.7 2.4 fusion.41
  158.1 2.4 fusion.41
  160.5 2.4 fusion.41
  162.9 2.4 fusion.41
  165.3 2.4 fusion.41
  167.7 2.4 fusion.41
  170.1 2.4 fusion.41
  172.5 2.4 fusion.41
  174.9 2.4 fusion.41
  177.3 2.4 fusion.41
  179.7 2.4 fusion.41
  182.1 2.4 fusion.41
  184.5 2.4 fusion.41
  186.9 2.4 fusion.41
  189.3 2.4 fusion.41
  191.7 2.4 fusion.41
  194.1 2.4 fusion.41
  196.5 2.4 fusion.41
  198.9 2.4 fusion.41
  201.3 2.4 fusion.41
  203.7 2.4 fusion.41
  206.2 2.4 fusion.41
  208.6 2.4 fusion.41
  212.3 7.2 %multiply_reduce_fusion.1 = (f32[64,1024]{1,0:T(8,128)S(1)}, f32[64,64,1024]{2,1,0:T(8,128)}) fusion(f32[64,64]{1,0:T(8,128)S(1)} %copy-done.3, bf16[64,64,128]{2,1,0:T(8,128)(2,1)S(1)} %bitcast.80, bf16[1024,128]{1,0:T(8,128)(2,1)S(1)} %copy-done), kind=kOutput, calls=%fused_computation.33 | convolution fusion | flops 1086259200 | bytes 18366464 | tf_op jit(solution)/shard_map/qjd,sd->qjs/dot_general | solution.py:72
  222.0 13.2 %all-reduce.3 = (f32[512]{0:T(512)S(1)}, f32[512]{0:T(512)S(1)}) all-reduce(f32[512]{0:T(512)S(1)} %dynamic-update-slice, f32[512]{0:T(512)S(1)} %dynamic-update-slice.1), channel_id=2, replica_groups=mesh['head'=4,'key'=8] {'key'}, use_global_device_ids=true, to_apply=%add | all-reduce | flops 1024 | bytes 8192
  235.6 4.0 %reduce-scatter.3.cloned.1.call-done = f32[64,1024]{1,0:T(8,128)} async-done(((f32[256,1024]{1,0:T(8,128)}), f32[64,1024]{1,0:T(8,128)}) %reduce-scatter.3.cloned.1.call-update) | async-done | bytes 262160 | tf_op jit(solution)/shard_map/reduce_scatter | solution.py:88
  240.7 8.3 %convolution_bitcast_fusion = f32[1024,128]{1,0:T(8,128)} fusion(bf16[64,64,128]{2,1,0:T(8,128)(2,1)S(1)} %bitcast.81, f32[64,64,1024]{2,1,0:T(8,128)} %get-tuple-element.469, f32[64,64]{1,0:T(8,128)S(1)} %broadcast_multiply_fusion, f32[64,1024]{1,0:T(8,128)S(1)} %multiply_select_fusion), kind=kOutput, calls=%fused_computation.35 | convolution fusion | flops 1090519040 | bytes 18628608 | tf_op jit(solution)/shard_map/qjs,qjd->sd/dot_general | solution.py:102
  249.3 7.2 %fusion.19 = f32[64,64,128]{2,1,0:T(8,128)S(1)} fusion(f32[64,64,1024]{2,1,0:T(8,128)} %get-tuple-element.469, f32[64,64]{1,0:T(8,128)S(1)} %broadcast_multiply_fusion, f32[64,1024]{1,0:T(8,128)S(1)} %multiply_select_fusion, bf16[1024,128]{1,0:T(8,128)(2,1)S(1)} %copy-done), kind=kOutput, calls=%fused_computation.36 | convolution fusion | flops 1090519040 | bytes 19415040 | tf_op jit(solution)/shard_map/qjs,sd->qjd/dot_general | solution.py:99
  256.5 2.5 copy.21
  259.7 7.6 %multiply_reduce_fusion = f32[64,64]{1,0:T(8,128)S(1)} fusion(f32[64,64,1024]{2,1,0:T(8,128)} %get-tuple-element.469, f32[64,1024]{1,0:T(8,128)S(1)} %multiply_select_fusion), kind=kLoop, calls=%fused_computation.31 | loop fusion | flops 12578816 | bytes 17055744 | tf_op jit(solution)/shard_map/reduce_sum | solution.py:103
  267.4 24.3 %all-reduce.2 = f32[64,64]{0,1:T(8,128)S(1)} all-reduce(f32[64,64]{0,1:T(8,128)S(1)} %copy.15), channel_id=8, replica_groups=mesh['head'=4,'key'=8] {'key'}, use_global_device_ids=true, to_apply=%region_17.18.clone | all-reduce | flops 4096 | bytes 32768
  292.3 39.3 %reduce-scatter.5.cloned.1.call-done = f32[64,1024]{1,0:T(8,128)} async-done(((f32[64,8192]{1,0:T(8,128)}), f32[64,1024]{1,0:T(8,128)}) %reduce-scatter.5.cloned.1.call-update) | async-done | bytes 262160 | tf_op jit(solution)/shard_map/reduce_scatter | solution.py:105
  (205 shorter events, 74.5 us)
Async XLA Ops:
  7.2 205.1 %copy-start = (bf16[1024,128]{1,0:T(8,128)(2,1)S(1)}, bf16[1024,128]{1,0:T(8,128)(2,1)}, u32[]{:S(2)}) copy-start(bf16[1024,128]{1,0:T(8,128)(2,1)} %param.19) | copy-start | bytes 786436
  7.2 232.4 %reduce-scatter.3.cloned.1.call-start = ((), (), s32[]{:S(2)}) async-start(), calls=%async_computation.2 | async-start | bytes 1310720 | tf_op jit(solution)/shard_map/reduce_scatter | solution.py:88
  133.9 78.1 %copy-start.1 = (bf16[64,8192]{1,0:T(8,128)(2,1)S(1)}, bf16[64,8192]{1,0:T(8,128)(2,1)}, u32[]{:S(2)}) copy-start(bf16[64,8192]{1,0:T(8,128)(2,1)} %param.18) | copy-start | bytes 3145732
  133.9 78.4 %copy-start.3 = (f32[64,64]{1,0:T(8,128)S(1)}, f32[64,64]{1,0:T(8,128)}, u32[]{:S(2)}) copy-start(f32[64,64]{1,0:T(8,128)} %param.20) | copy-start | bytes 49156
  210.9 1.0 copy-start.2
  210.9 8.6 %copy-start.4 = (s32[256]{0:T(256)S(1)}, s32[256]{0:T(256)}, u32[]{:S(2)}) copy-start(s32[256]{0:T(256)} %get-tuple-element.780) | copy-start | bytes 3076
  211.0 8.7 %copy-start.5 = (s32[256]{0:T(256)S(1)}, s32[256]{0:T(256)}, u32[]{:S(2)}) copy-start(s32[256]{0:T(256)} %get-tuple-element.782) | copy-start | bytes 3076
  211.0 8.7 %copy-start.6 = (u32[32]{0:T(128)S(1)}, u32[32]{0:T(128)}, u32[]{:S(2)}) copy-start(u32[32]{0:T(128)} %constant.136) | copy-start | bytes 388
  211.0 28.6 %copy-start.7 = (f32[64]{0:T(128)S(1)}, f32[64]{0:T(128)}, u32[]{:S(2)}) copy-start(f32[64]{0:T(128)} %param.21) | copy-start | bytes 772
  212.0 80.4 %all-reduce.6.cloned.1.call-start = ((), (), s32[]{:S(2)}) async-start(), calls=%async_computation.4 | async-start | bytes 1048576 | tf_op jit(solution)/shard_map/psum | solution.py:108
  249.1 82.5 %reduce-scatter.5.cloned.1.call-start = ((), (), s32[]{:S(2)}) async-start(), calls=%async_computation.3 | async-start | bytes 2359296 | tf_op jit(solution)/shard_map/reduce_scatter | solution.py:105
Sparse Core Ops, SparseCore 0:
  212.1 27.4 reduce-scatter.2
  249.2 36.9 all-reduce.5
  290.4 41.1 reduce-scatter.4
where the time goes:
time: 343 us; the launch traced here: 340 us
  matrix products  165 us (48%)
  blocking collectives  57.5 us (17%)
  other arithmetic  46.5 us (14%)
  waiting for transfers between devices  43.3 us (13%)
  between operations  15.2 us (4%)
  local copies, waits for them, and re-layouts  10.4 us (3%)
    dot_general x64, matrix products, main_scores(): jnp.einsum('qd,sd->qs', q_rows, k_latent, preferred_element_type=jnp.floa...  142 us
    reduce_scatter x1, waiting for transfers between devices, shards(): lax.psum_scatter(query_part, 'key', scatter_dimension=1, tiled=True)  39.3 us
    unnamed x2, blocking collectives  37.5 us
    reduce_sum x33, other arithmetic, local_stats(): return (highest, jnp.sum(exponents, axis=-1))  36.5 us
    all_gather x2, blocking collectives, joined(): everything = jax.tree.map(lambda part: lax.all_gather(part, axis), x)  20 us
    dot_general x1, matrix products, shards(): jnp.einsum('qjs,qjd->sd', head_grad, q_heads, preferred_element_type=jnp....  8.33 us
    reduce_sum x1, other arithmetic, shards(): weight_part = jnp.sum(grad_scores[:, None, :] * rectified, axis=2)  7.61 us
    dot_general x1, matrix products, shards(): jnp.einsum('qjd,sd->qjs', q_heads, k_index, preferred_element_type=jnp.fl...  7.25 us
  transfers between devices with their start and end apart: 3, of which 2 were waited for; matrix products, arithmetic and copies ran while one was open for 8% of the time, Pallas kernels for 0%

commit v1 on v0

v1 whole, which is shorter than its diff:
```python
import functools
import math

import jax
import jax.numpy as jnp
from jax import lax
from jax.experimental import pallas as pl
from jax.experimental.pallas import tpu as pltpu
from jax.sharding import PartitionSpec as P

H = 128
QK_DIM = 192
LOW = -1e30
FLOOR = -1e29
LOG2E = math.log2(math.e)
NT = (((1,), (1,)), ((), ()))
VMEM_LIMIT = 56 * 1024 * 1024


def main_kernel(heads_step, q_ref, k_ref, start_ref, pos_ref, e_ref, high_ref, sum_ref, bias):
    step = pl.program_id(0)
    keys_here = k_ref.shape[0]
    factor = LOG2E / math.sqrt(QK_DIM)

    @pl.when(step == 0)
    def _():
        position = lax.broadcasted_iota(jnp.int32, bias.shape, 0) + lax.axis_index("key") * keys_here
        seen = (position >= start_ref[...]) & (position <= pos_ref[...])
        bias[...] = jnp.where(seen, 0.0, LOW)

    for i in range(heads_step):
        scores = lax.dot_general(k_ref[...], q_ref[i], NT, preferred_element_type=jnp.float32) + bias[...]
        high = jnp.maximum(jnp.max(scores, axis=0, keepdims=True), FLOOR)
        exponents = jnp.exp2((scores - high) * factor)
        e_ref[i] = exponents
        high_ref[pl.ds(step * heads_step + i, 1), :] = high
        sum_ref[pl.ds(step * heads_step + i, 1), :] = jnp.sum(exponents, axis=0, keepdims=True)


def target_kernel(e_ref, c_ref, out_ref):
    heads = e_ref.shape[0]
    total = e_ref[0] * c_ref[0:1, :]
    for h in range(1, heads):
        total = total + e_ref[h] * c_ref[h : h + 1, :]
    out_ref[...] = total.T


def stacked(q_ref, group, heads, dim):
    width = heads * dim
    block = q_ref[:, pl.ds(pl.multiple_of(group * width, width), width)]
    return jnp.concatenate([block[:, i * dim : (i + 1) * dim] for i in range(heads)], axis=0)


def index_kernel(q_ref, k_ref, w_ref, start_ref, pos_ref, scores_ref, high_ref, sum_ref):
    groups, rows, heads = w_ref.shape
    keys_here, dim = k_ref.shape
    scores_ref[...] = jnp.zeros_like(scores_ref)

    def lap(group, carry):
        dots = lax.dot_general(
            stacked(q_ref, group, heads, dim), k_ref[...], NT, preferred_element_type=jnp.float32
        )
        weights = w_ref[group]
        total = scores_ref[...]
        for i in range(heads):
            total = total + weights[:, i : i + 1] * jnp.maximum(dots[i * rows : (i + 1) * rows], 0.0)
        scores_ref[...] = total
        return carry

    lax.fori_loop(0, groups, lap, 0)
    position = lax.broadcasted_iota(jnp.int32, (rows, keys_here), 1) + lax.axis_index("key") * keys_here
    seen = (position >= start_ref[...]) & (position <= pos_ref[...])
    scores = jnp.where(seen, scores_ref[...] * (1.0 / math.sqrt(dim)), LOW)
    scores_ref[...] = scores
    high = jnp.maximum(jnp.max(scores, axis=1, keepdims=True), FLOOR)
    high_ref[...] = high
    sum_ref[...] = jnp.sum(jnp.exp(scores - high), axis=1, keepdims=True)


def grad_kernel(q_ref, k_ref, w_ref, scores_ref, target_ref, high_ref, sum_ref, loss_ref,
                query_ref, key_ref, weight_ref, key_t, grads):
    groups, rows, heads = w_ref.shape
    keys_here, dim = k_ref.shape
    scale = 1.0 / math.sqrt(dim)
    scores = scores_ref[...]
    probs = jnp.exp(scores - high_ref[...]) / sum_ref[...]
    grads[...] = jnp.where(
        scores > FLOOR, loss_ref[...] * (probs - target_ref[...] * (1.0 / H)), 0.0
    )
    key_t[...] = jnp.zeros_like(key_t)

    def lap(group, carry):
        queries = stacked(q_ref, group, heads, dim)
        dots = lax.dot_general(queries, k_ref[...], NT, preferred_element_type=jnp.float32)
        weights = w_ref[group] * scale
        pieces, sums = [], []
        for i in range(heads):
            own = dots[i * rows : (i + 1) * rows]
            g = grads[...]
            pieces.append(jnp.where(own > 0.0, g * weights[:, i : i + 1], 0.0).astype(jnp.bfloat16))
            sums.append(jnp.sum(g * jnp.maximum(own, 0.0), axis=1, keepdims=True))
        head_grad = jnp.concatenate(pieces, axis=0)
        part = jnp.dot(head_grad, k_ref[...], preferred_element_type=jnp.float32)
        query_ref[group] = jnp.concatenate(
            [part[i * rows : (i + 1) * rows] for i in range(heads)], axis=1
        )
        key_t[...] += jnp.dot(queries.T, head_grad, preferred_element_type=jnp.float32)
        weight_ref[group] = jnp.concatenate(sums, axis=1) * scale
        return carry

    lax.fori_loop(0, groups, lap, 0)
    key_ref[...] = key_t[...].T


def shards(q_latent, k_latent, q_index, k_index, head_weight, loss_weight, query_pos, key_start):
    heads_here, queries, lat = q_latent.shape
    keys_here = k_latent.shape[0]
    rows, index_width = q_index.shape
    index_heads = head_weight.shape[1]
    dim = k_index.shape[1]
    key_devices = lax.axis_size("key")
    group_heads = index_heads // key_devices
    factor = LOG2E / math.sqrt(QK_DIM)
    params = pltpu.CompilerParams(vmem_limit_bytes=VMEM_LIMIT)
    f32 = jnp.float32

    heads_step = 2
    whole = lambda *shape: pl.BlockSpec(shape, lambda *_: (0,) * len(shape))
    exponents, main_high, main_sum = pl.pallas_call(
        functools.partial(main_kernel, heads_step),
        grid=(heads_here // heads_step,),
        in_specs=[
            pl.BlockSpec((heads_step, queries, lat), lambda h: (h, 0, 0)),
            whole(keys_here, lat),
            whole(1, queries),
            whole(1, queries),
        ],
        out_specs=[
            pl.BlockSpec((heads_step, keys_here, queries), lambda h: (h, 0, 0)),
            whole(heads_here, queries),
            whole(heads_here, queries),
        ],
        out_shape=[
            jax.ShapeDtypeStruct((heads_here, keys_here, queries), f32),
            jax.ShapeDtypeStruct((heads_here, queries), f32),
            jax.ShapeDtypeStruct((heads_here, queries), f32),
        ],
        scratch_shapes=[pltpu.VMEM((keys_here, queries), f32)],
        compiler_params=params,
    )(q_latent, k_latent, key_start[None, :], query_pos[None, :])

    row_start = lax.axis_index("head") * rows
    own_pos = lax.dynamic_slice_in_dim(query_pos, row_start, rows)[:, None]
    own_start = lax.dynamic_slice_in_dim(key_start, row_start, rows)[:, None]
    weights = head_weight.reshape(rows, key_devices, group_heads).transpose(1, 0, 2)
    index_scores, index_high, index_sum = pl.pallas_call(
        index_kernel,
        out_shape=[
            jax.ShapeDtypeStruct((rows, keys_here), f32),
            jax.ShapeDtypeStruct((rows, 1), f32),
            jax.ShapeDtypeStruct((rows, 1), f32),
        ],
        compiler_params=params,
    )(q_index, k_index, weights, own_start, own_pos)

    stats = jnp.concatenate(
        [main_high.reshape(-1), main_sum.reshape(-1), index_high.reshape(-1), index_sum.reshape(-1)]
    )
    stats = lax.all_gather(stats, "key")
    size = heads_here * queries
    high_all = stats[:, :size]
    high = jnp.max(high_all, axis=0)
    total = jnp.sum(stats[:, size : 2 * size] * jnp.exp2((high_all - high) * factor), axis=0)
    coef = jnp.exp2((main_high.reshape(-1) - high) * factor) / total
    coef = coef.reshape(heads_here, queries)
    ihigh_all = stats[:, 2 * size : 2 * size + rows]
    ihigh = jnp.max(ihigh_all, axis=0)
    itotal = jnp.sum(stats[:, 2 * size + rows :] * jnp.exp(ihigh_all - ihigh), axis=0)

    tile = 128
    summed = pl.pallas_call(
        target_kernel,
        grid=(keys_here // tile,),
        in_specs=[
            pl.BlockSpec((heads_here, tile, queries), lambda s: (0, s, 0)),
            whole(heads_here, queries),
        ],
        out_specs=pl.BlockSpec((queries, tile), lambda s: (0, s)),
        out_shape=jax.ShapeDtypeStruct((queries, keys_here), f32),
        compiler_params=params,
    )(exponents, coef)
    target = lax.psum_scatter(summed, "head", scatter_dimension=0, tiled=True)

    query_part, key_part, weight_part = pl.pallas_call(
        grad_kernel,
        out_shape=[
            jax.ShapeDtypeStruct((key_devices, rows, index_width // key_devices), f32),
            jax.ShapeDtypeStruct((keys_here, dim), f32),
            jax.ShapeDtypeStruct((key_devices, rows, group_heads), f32),
        ],
        scratch_shapes=[pltpu.VMEM((dim, keys_here), f32), pltpu.VMEM((rows, keys_here), f32)],
        compiler_params=params,
    )(q_index, k_index, weights, index_scores, target, ihigh[:, None], itotal[:, None], loss_weight[:, None])

    grad_query = lax.psum_scatter(query_part, "key", scatter_dimension=0, tiled=False)
    grad_weight = lax.psum_scatter(weight_part, "key", scatter_dimension=0, tiled=False)
    grad_key = lax.psum(key_part, "head")
    return (grad_query, grad_key, grad_weight)


def solution(mesh):
    return jax.shard_map(
        shards,
        mesh=mesh,
        in_specs=(
            P("head", None, None),
            P("key", None),
            P("head", None),
            P("key", None),
            P("head", None),
            P("head"),
            P(),
            P(),
        ),
        out_specs=(P("head", "key"), P("key", None), P("head", "key")),
        check_vma=False,
    )
```

time: 343 us -> 256 us (0.75)
  matrix products: 165 us -> 0 us
  waiting for transfers between devices: 43.3 us -> 142 us
  Pallas kernels: 0 us -> 56.5 us
  blocking collectives: 57.5 us -> 11.3 us
  other arithmetic: 46.5 us -> 3.43 us
  local copies, waits for them, and re-layouts: 10.4 us -> 26.8 us
    dot_general x67 -> x0, matrix products: 165 us -> none  [the longest x64 142 us: main_scores(): jnp.einsum('qd,sd->qs', q_rows, k_latent, preferred_element_type=jnp.floa...]
    pallas_call x0 -> x4, Pallas kernels: none -> 56.5 us  [the longest x1 26.8 us: shards(): pl.pallas_call(functools.partial(main_kernel, heads_step), grid=(heads_he...]
    reduce_sum x34 -> x2, other arithmetic: 44.1 us -> 0.21 us  [the longest x1 0.12 us: shards(): jnp.sum(stats[:, size:2 * size] * jnp.exp2((high_all - high) * factor), a...]
    psum x1, waiting for transfers between devices: 0.01 us -> 39.8 us  [shards(): grad_key = lax.psum(key_part, 'head')]
    unnamed x2 -> x0, blocking collectives: 37.5 us -> none
    reduce_scatter x1 -> x2, waiting for transfers between devices: 39.3 us -> 76.1 us  [the longest x1 45 us: shards(): lax.psum_scatter(query_part, 'key', scatter_dimension=0, tiled=False)]
    reduce_scatter x1, waiting for transfers between devices: 3.99 us -> 25.3 us  [shards(): target = lax.psum_scatter(summed, 'head', scatter_dimension=0, tiled=True)]
    unnamed x24 -> x13, local copies, waits for them, and re-layouts: 6.81 us -> 21.6 us
  transfers between devices with their start and end apart: 3 -> 4, of which waited for: 2 -> 4; matrix products, arithmetic and copies ran while one was open for 8% -> 1% of each run, Pallas kernels for 0% -> 0%
where the time goes in v1:
time: 256 us; the launch traced here: 255 us
  waiting for transfers between devices  142 us (55%)
  Pallas kernels  56.5 us (22%)
  local copies, waits for them, and re-layouts  26.8 us (10%)
  between operations  13.8 us (5%)
  blocking collectives  11.3 us (4%)
  other arithmetic  3.43 us (1%)
    reduce_scatter x1, waiting for transfers between devices, shards(): lax.psum_scatter(query_part, 'key', scatter_dimension=0, tiled=False)  45 us
    psum x1, waiting for transfers between devices, shards(): grad_key = lax.psum(key_part, 'head')  39.8 us
    reduce_scatter x1, waiting for transfers between devices, shards(): lax.psum_scatter(weight_part, 'key', scatter_dimension=0, tiled=False)  31.1 us
    pallas_call x1, Pallas kernels, shards(): pl.pallas_call(functools.partial(main_kernel, heads_step), grid=(heads_he...  26.8 us
    reduce_scatter x1, waiting for transfers between devices, shards(): target = lax.psum_scatter(summed, 'head', scatter_dimension=0, tiled=True)  25.3 us
    unnamed x13, local copies, waits for them, and re-layouts  21.6 us
    pallas_call x1, Pallas kernels, shards(): pl.pallas_call(target_kernel, grid=(keys_here // tile,), in_specs=[pl.Blo...  13.2 us
    all_gather x1, blocking collectives, shards(): stats = lax.all_gather(stats, 'key')  11.3 us
  transfers between devices with their start and end apart: 4, of which 4 were waited for; matrix products, arithmetic and copies ran while one was open for 1% of the time, Pallas kernels for 0%

profile of v1, /device:TPU:0, one launch (start us, length us, event | category | flops | bytes accessed | tf_op | source)
XLA Modules:
  0.0 254.5 jit_solution(691519260454713538)
XLA Ops:
  7.2 0.0 reduce-scatter.4.cloned.1.call-start
  7.2 0.8 dynamic-slice_bitcast_fusion
  8.0 0.7 copy.31.start_ref
  8.7 0.7 copy.32.pos_ref
  9.4 0.8 copy.29
  10.2 0.8 copy.30
  11.1 5.8 %shard_map.103 = (f32[64,1024]{1,0:T(8,128)}, f32[64,1]{1,0:T(8,128)}, f32[64,1]{1,0:T(8,128)}) custom-call(bf16[64,8192]{1,0:T(8,128)(2,1)} %q_ref.4, bf16[1024,128]{1,0:T(8,128)(2,1)} %k_ref.4, f32[8,64,8]{2,1,0:T(8,128)} %bitcast.24, s32[64,1]{1,0:T(8,128)} %copy.31.start_ref, s32[64,1]{1,0:T(8,128)} %copy.32.pos_ref), custom_call_target="tpu_custom_call" | custom-call | tf_op jit(solution)/shard_map/pallas_call | solution.py:156
  16.9 0.9 reduce
  17.8 0.9 reduce.1
  18.7 0.0 copy-start
  18.7 14.4 %copy.33.q_ref = bf16[32,256,576]{2,1,0:T(8,128)(2,1)} copy(bf16[32,256,576]{1,2,0:T(8,128)(2,1)} %param.8) | data formatting | bytes 18874368 | tf_op args[0]
  33.1 0.0 copy-done
  33.1 1.4 copy.34.k_ref
  34.5 26.8 %shard_map.104 = (f32[32,1024,256]{2,1,0:T(8,128)}, f32[32,256]{1,0:T(8,128)}, f32[32,256]{1,0:T(8,128)}) custom-call(bf16[32,256,576]{2,1,0:T(8,128)(2,1)} %copy.33.q_ref, bf16[1024,576]{1,0:T(8,128)(2,1)} %copy.34.k_ref, s32[1,256]{1,0:T(1,128)} %bitcast.33, s32[1,256]{1,0:T(1,128)} %bitcast.34), custom_call_target="tpu_custom_call" | custom-call | tf_op jit(solution)/shard_map/pallas_call | solution.py:129
  61.3 0.8 copy.40
  62.1 0.8 copy.41
  62.9 0.1 concatenate.3
  63.0 11.3 %all-gather.1 = f32[8,1,16512]{2,1,0:T(1,128)S(1)} all-gather(f32[1,1,16512]{2,1,0:T(1,128)S(1)} %reshape.33), channel_id=2, replica_groups=mesh['head'=4,'key'=8] {'key'}, dimensions={0}, use_global_device_ids=true | all-gather | bytes 594432 | tf_op jit(solution)/shard_map/all_gather | solution.py:169
  74.4 0.1 slice_reduce_fusion
  74.5 0.1 fusion
  74.6 1.4 exponential_divide_fusion.c_ref
  76.0 0.0 copy-start.1
  76.0 13.2 %shard_map.105 = f32[256,1024]{1,0:T(8,128)} custom-call(f32[32,1024,256]{2,1,0:T(8,128)} %get-tuple-element.13.e_ref, f32[32,256]{1,0:T(8,128)} %exponential_divide_fusion.c_ref), custom_call_target="tpu_custom_call" | custom-call | tf_op jit(solution)/shard_map/pallas_call | solution.py:181
  89.2 0.0 reduce-scatter.4.cloned.1.call-update
  89.3 0.0 reduce-scatter.8.cloned.1.call-start
  89.3 0.1 fusion.1
  89.4 0.7 copy.36.sum_ref
  90.1 0.7 copy.35.high_ref
  90.8 0.0 copy-done.1
  90.8 0.7 copy.37.loss_ref
  91.5 25.3 %reduce-scatter.4.cloned.1.call-done.target_ref = f32[64,1024]{1,0:T(8,128)} async-done(((f32[256,1024]{1,0:T(8,128)}), f32[64,1024]{1,0:T(8,128)}) %reduce-scatter.4.cloned.1.call-update) | async-done | bytes 262160 | tf_op jit(solution)/shard_map/reduce_scatter | solution.py:192
  116.8 10.6 %shard_map.106 = (f32[8,64,1024]{2,1,0:T(8,128)}, f32[1024,128]{1,0:T(8,128)}, f32[8,64,8]{2,1,0:T(8,128)}) custom-call(bf16[64,8192]{1,0:T(8,128)(2,1)} %q_ref.4, bf16[1024,128]{1,0:T(8,128)(2,1)} %k_ref.4, f32[8,64,8]{2,1,0:T(8,128)} %bitcast.25, f32[64,1024]{1,0:T(8,128)} %get-tuple-element.12.scores_ref, ...), custom_call_target="tpu_custom_call" | custom-call | tf_op jit(solution)/shard_map/pallas_call | solution.py:194
  127.5 0.0 reduce-scatter.8.cloned.1.call-update
  127.5 0.0 all-reduce.2.cloned.1.call-start
  127.5 0.7 all-reduce.2.cloned.1.call-update
  128.2 0.0 reduce-scatter.6.cloned.1.call-start
  128.3 0.5 reduce-scatter.6.cloned.1.call-update
  128.8 31.1 %reduce-scatter.8.cloned.1.call-done = f32[1,64,8]{2,1,0:T(8,128)} async-done(((f32[8,64,8]{2,1,0:T(8,128)}), f32[1,64,8]{2,1,0:T(8,128)}) %reduce-scatter.8.cloned.1.call-update) | async-done | bytes 2064 | tf_op jit(solution)/shard_map/reduce_scatter | solution.py:206
  159.9 1.4 copy.38
  161.4 39.8 %all-reduce.2.cloned.1.call-done = f32[1024,128]{1,0:T(8,128)} async-done(((f32[1024,128]{1,0:T(8,128)}), f32[1024,128]{1,0:T(8,128)}) %all-reduce.2.cloned.1.call-update) | async-done | bytes 524304 | tf_op jit(solution)/shard_map/psum | solution.py:207
  201.2 45.0 %reduce-scatter.6.cloned.1.call-done = f32[1,64,1024]{2,1,0:T(8,128)} async-done(((f32[8,64,1024]{2,1,0:T(8,128)}), f32[1,64,1024]{2,1,0:T(8,128)}) %reduce-scatter.6.cloned.1.call-update) | async-done | bytes 262160 | tf_op jit(solution)/shard_map/reduce_scatter | solution.py:205
  246.1 1.9 copy.45
  (5 shorter events, 0.1 us)
Async XLA Ops:
  7.2 109.7 %reduce-scatter.4.cloned.1.call-start = ((), (), s32[]{:S(2)}) async-start(), calls=%async_computation.3 | async-start | bytes 1310720 | tf_op jit(solution)/shard_map/reduce_scatter | solution.py:192
  18.7 14.4 %copy-start = (bf16[1024,576]{0,1:T(8,128)(2,1)S(1)}, bf16[1024,576]{0,1:T(8,128)(2,1)}, u32[]{:S(2)}) copy-start(bf16[1024,576]{0,1:T(8,128)(2,1)} %param.9) | copy-start | bytes 3538948
  76.0 14.8 %copy-start.1 = (f32[64]{0:T(128)S(1)}, f32[64]{0:T(128)}, u32[]{:S(2)}) copy-start(f32[64]{0:T(128)} %param.13) | copy-start | bytes 772
  89.3 70.7 %reduce-scatter.8.cloned.1.call-start = ((), (), s32[]{:S(2)}) async-start(), calls=%async_computation.6 | async-start | bytes 294912 | tf_op jit(solution)/shard_map/reduce_scatter | solution.py:206
  127.5 73.7 %all-reduce.2.cloned.1.call-start = ((), (), s32[]{:S(2)}) async-start(), calls=%async_computation.5 | async-start | bytes 1048576 | tf_op jit(solution)/shard_map/psum | solution.py:207
  128.2 117.9 %reduce-scatter.6.cloned.1.call-start = ((), (), s32[]{:S(2)}) async-start(), calls=%async_computation.4 | async-start | bytes 2359296 | tf_op jit(solution)/shard_map/reduce_scatter | solution.py:205
Sparse Core Ops, SparseCore 0:
  89.4 27.4 reduce-scatter.3
  127.6 32.2 reduce-scatter.7
  162.9 38.2 all-reduce.1
  204.9 41.1 reduce-scatter.5

commit v2 on v0

v2 whole, which is shorter than its diff:
```python
import math

import jax
import jax.numpy as jnp
from jax import lax
from jax.experimental import pallas as pl
from jax.experimental.pallas import tpu as pltpu
from jax.sharding import PartitionSpec as P

H = 128
QK_DIM = 192
LOW = -1e30
FLOOR = -1e29
LOG2E = math.log2(math.e)
NT = (((1,), (1,)), ((), ()))
VMEM_LIMIT = 60 * 1024 * 1024


def stacked(q_ref, group, heads, dim):
    width = heads * dim
    block = q_ref[:, pl.ds(pl.multiple_of(group * width, width), width)]
    return jnp.concatenate([block[:, i * dim : (i + 1) * dim] for i in range(heads)], axis=0)


def kernel(q_hbm, k_ref, start_row, pos_row, qi_ref, ki_ref, w_ref, start_col, pos_col, loss_ref,
           gq_ref, gk_ref, gw_ref,
           e, bias, raw_a, raw_b, q_first, q_last, q_pair, stats, stats_in, coef,
           iscores, istats, istats_in, t_send, t_in, grads, key_t, key_sum, key_in,
           part_send, part_in,
           q_sem, st_send, st_recv, is_send, is_recv, tg_send, tg_recv, pt_send, pt_recv,
           kr_send, kr_recv, kg_send, kg_recv):
    heads = q_hbm.shape[0]
    keys_here, queries = bias.shape
    groups, rows, group_heads = w_ref.shape
    dim = ki_ref.shape[1]
    width = group_heads * dim
    key_devices, head_devices = lax.axis_size("key"), lax.axis_size("head")
    my_key, my_head = lax.axis_index("key"), lax.axis_index("head")
    factor = LOG2E / math.sqrt(QK_DIM)
    index_scale = 1.0 / math.sqrt(dim)
    first_key = my_key * keys_here
    f32 = jnp.float32

    def peer(axis, offset):
        return lax.rem(lax.axis_index(axis) + offset, lax.axis_size(axis))

    def send(src, dst, send_sem, recv_sem, axis, offset):
        return pltpu.make_async_remote_copy(
            src_ref=src, dst_ref=dst, send_sem=send_sem, recv_sem=recv_sem,
            device_id={axis: peer(axis, offset)}, device_id_type=pl.DeviceIdType.MESH)

    pairs = (heads - 2) // 2
    copy_first = pltpu.make_async_copy(q_hbm.at[0], q_first, q_sem.at[2])
    copy_last = pltpu.make_async_copy(q_hbm.at[heads - 1], q_last, q_sem.at[3])

    def copy_pair(i):
        slot = lax.rem(i, 2)
        return pltpu.make_async_copy(q_hbm.at[pl.ds(2 * i + 1, 2)], q_pair.at[slot], q_sem.at[slot])

    copy_first.start()
    copy_last.start()
    copy_pair(0).start()

    barrier = pltpu.get_barrier_semaphore()
    for axis, count in (("key", key_devices), ("head", head_devices)):
        for offset in range(1, count):
            pl.semaphore_signal(barrier, inc=1, device_id={axis: peer(axis, offset)},
                                device_id_type=pl.DeviceIdType.MESH)

    position = lax.broadcasted_iota(jnp.int32, bias.shape, 0) + first_key
    bias[...] = jnp.where((position >= start_row[...]) & (position <= pos_row[...]), 0.0, LOW)

    chunk = 256

    def stage(query, dst, src, src_high, src_head):
        high = jnp.full((1, queries), FLOOR, f32)
        total = jnp.zeros((1, queries), f32)
        for c in range(0, keys_here, chunk):
            if query is not None:
                scores = jnp.dot(k_ref[c : c + chunk], query[...], preferred_element_type=f32)
                scores = scores + bias[c : c + chunk]
                dst[c : c + chunk] = scores
                high = jnp.maximum(high, jnp.max(scores, axis=0, keepdims=True))
            if src is not None:
                exponents = jnp.exp2((src[c : c + chunk] - src_high) * factor)
                e[src_head, c : c + chunk] = exponents
                total = total + jnp.sum(exponents, axis=0, keepdims=True)
        if src is not None:
            stats[0, pl.ds(src_head, 1)] = src_high
            stats[1, pl.ds(src_head, 1)] = total
        return high

    copy_first.wait()
    high = stage(q_first, raw_a, None, None, None)

    def pair(i, high):
        copy_pair(i).wait()

        @pl.when(i + 1 < pairs)
        def _():
            copy_pair(i + 1).start()

        slot = lax.rem(i, 2)
        high = stage(q_pair.at[slot, 0], raw_b, raw_a, high, 2 * i)
        return stage(q_pair.at[slot, 1], raw_a, raw_b, high, 2 * i + 1)

    high = lax.fori_loop(0, pairs, pair, high)
    copy_last.wait()
    high = stage(q_last, raw_b, raw_a, high, heads - 2)
    stage(None, None, raw_b, high, heads - 1)

    pl.semaphore_wait(barrier, key_devices + head_devices - 2)

    def send_stats(d):
        return send(stats, stats_in.at[d - 1], st_send.at[d - 1], st_recv.at[d - 1], "key", d)

    for d in range(1, key_devices):
        send_stats(d).start()

    iscores[...] = jnp.zeros_like(iscores)

    def index_lap(group, carry):
        dots = lax.dot_general(stacked(qi_ref, group, group_heads, dim), ki_ref[...], NT,
                               preferred_element_type=f32)
        weights = w_ref[group]
        total = iscores[...]
        for i in range(group_heads):
            total = total + weights[:, i : i + 1] * jnp.maximum(dots[i * rows : (i + 1) * rows], 0.0)
        iscores[...] = total
        return carry

    lax.fori_loop(0, groups, index_lap, 0)
    position = lax.broadcasted_iota(jnp.int32, (rows, keys_here), 1) + first_key
    seen = (position >= start_col[...]) & (position <= pos_col[...])
    scores = jnp.where(seen, iscores[...] * index_scale, LOW)
    iscores[...] = scores
    high = jnp.maximum(jnp.max(scores, axis=1, keepdims=True), FLOOR)
    total = jnp.sum(jnp.exp(scores - high), axis=1, keepdims=True)
    lane = lax.broadcasted_iota(jnp.int32, istats.shape, 1)
    istats[...] = jnp.where(lane == 0, high, jnp.where(lane == 1, total, 0.0))

    def send_istats(d):
        return send(istats, istats_in.at[d - 1], is_send.at[d - 1], is_recv.at[d - 1], "key", d)

    for d in range(1, key_devices):
        send_istats(d).start()

    for d in range(1, key_devices):
        send_stats(d).wait()
    high = stats[0]
    for d in range(1, key_devices):
        high = jnp.maximum(high, stats_in[d - 1, 0])
    own = jnp.exp2((stats[0] - high) * factor)
    total = stats[1] * own
    for d in range(1, key_devices):
        total = total + stats_in[d - 1, 1] * jnp.exp2((stats_in[d - 1, 0] - high) * factor)
    coef[...] = own / total

    tile = 128
    halves = t_send.shape[0]
    half = keys_here // halves

    def send_target(d, part):
        return send(t_send.at[part, peer("head", d)], t_in.at[d - 1, part],
                    tg_send.at[d - 1, part], tg_recv.at[d - 1, part], "head", d)

    for part in range(halves):
        for c in range(0, half, tile):
            at = part * half + c
            total = e[0, at : at + tile] * coef[0:1]
            for h in range(1, heads):
                total = total + e[h, at : at + tile] * coef[h : h + 1]
            across = total.T
            for z in range(head_devices):
                t_send[part, z, :, c : c + tile] = across[z * rows : (z + 1) * rows]
        for d in range(1, head_devices):
            send_target(d, part).start()

    for d in range(1, key_devices):
        send_istats(d).wait()
    high = istats[:, 0:1]
    for d in range(1, key_devices):
        high = jnp.maximum(high, istats_in[d - 1, :, 0:1])
    total = istats[:, 1:2] * jnp.exp(istats[:, 0:1] - high)
    for d in range(1, key_devices):
        total = total + istats_in[d - 1, :, 1:2] * jnp.exp(istats_in[d - 1, :, 0:1] - high)
    scores = iscores[...]
    iscores[...] = jnp.exp(scores - high) / total

    for part in range(halves):
        for d in range(1, head_devices):
            send_target(d, part).wait()
        span = slice(part * half, (part + 1) * half)
        target = t_send[part, my_head]
        for d in range(1, head_devices):
            target = target + t_in[d - 1, part]
        grads[:, span] = jnp.where(
            seen[:, span], loss_ref[...] * (iscores[:, span] - target * (1.0 / H)), 0.0)

    key_t[...] = jnp.zeros_like(key_t)

    def send_part(d):
        return send(part_send.at[d], part_in.at[d - 1], pt_send.at[d - 1], pt_recv.at[d - 1], "key", d)

    def grad_lap(lap, carry):
        d = key_devices - 1 - lap
        group = peer("key", d)
        stack = stacked(qi_ref, group, group_heads, dim)
        dots = lax.dot_general(stack, ki_ref[...], NT, preferred_element_type=f32)
        weights = w_ref[group] * index_scale
        pieces, sums = [], []
        for i in range(group_heads):
            own = dots[i * rows : (i + 1) * rows]
            g = grads[...]
            pieces.append(jnp.where(own > 0.0, g * weights[:, i : i + 1], 0.0).astype(jnp.bfloat16))
            sums.append(jnp.sum(g * jnp.maximum(own, 0.0), axis=1, keepdims=True))
        head_grad = jnp.concatenate(pieces, axis=0)
        part = jnp.dot(head_grad, ki_ref[...], preferred_element_type=f32)
        for i in range(group_heads):
            part_send[d, :, i * dim : (i + 1) * dim] = part[i * rows : (i + 1) * rows]
        lane = lax.broadcasted_iota(jnp.int32, (rows, 128), 1)
        extra = jnp.zeros((rows, 128), f32)
        for i in range(group_heads):
            extra = jnp.where(lane == i, sums[i], extra)
        part_send[d, :, width:] = extra * index_scale

        @pl.when(d > 0)
        def _():
            send_part(d).start()

        key_t[...] += jnp.dot(stack.T, head_grad, preferred_element_type=f32)
        return carry

    lax.fori_loop(0, key_devices, grad_lap, 0)

    block = keys_here // head_devices
    key_sum[...] = key_t[...].T.reshape(head_devices, block, dim)

    def reduce_key(d):
        return send(key_sum.at[peer("head", d)], key_in.at[d - 1],
                    kr_send.at[d - 1], kr_recv.at[d - 1], "head", d)

    def gather_key(d):
        return send(gk_ref.at[my_head], gk_ref.at[my_head],
                    kg_send.at[d - 1], kg_recv.at[d - 1], "head", d)

    for d in range(1, head_devices):
        reduce_key(d).start()
    for d in range(1, head_devices):
        reduce_key(d).wait()
    total = key_sum[my_head]
    for d in range(1, head_devices):
        total = total + key_in[d - 1]
    gk_ref[my_head] = total
    for d in range(1, head_devices):
        gather_key(d).start()

    gq_ref[...] = part_send[0, :, :width]
    gw_ref[...] = part_send[0, :, width : width + group_heads]
    for d in range(1, key_devices):
        send_part(d).wait()
        gq_ref[...] += part_in[d - 1, :, :width]
        gw_ref[...] += part_in[d - 1, :, width : width + group_heads]
    for d in range(1, head_devices):
        gather_key(d).wait()


def shards(q_latent, k_latent, q_index, k_index, head_weight, loss_weight, query_pos, key_start):
    heads_here, queries, lat = q_latent.shape
    keys_here = k_latent.shape[0]
    rows, index_width = q_index.shape
    index_heads = head_weight.shape[1]
    dim = k_index.shape[1]
    nk, nh = lax.axis_size("key"), lax.axis_size("head")
    group_heads = index_heads // nk
    width = index_width // nk
    f32, bf16 = jnp.float32, jnp.bfloat16
    row_start = lax.axis_index("head") * rows
    own_pos = lax.dynamic_slice_in_dim(query_pos, row_start, rows)[:, None]
    own_start = lax.dynamic_slice_in_dim(key_start, row_start, rows)[:, None]
    weights = head_weight.reshape(rows, nk, group_heads).transpose(1, 0, 2)
    halves = 2
    dma = lambda *shape: pltpu.SemaphoreType.DMA(shape)
    in_vmem = pl.BlockSpec(memory_space=pltpu.VMEM)
    grad_query, grad_key, grad_weight = pl.pallas_call(
        kernel,
        in_specs=[pl.BlockSpec(memory_space=pl.ANY)] + [in_vmem] * 9,
        out_specs=[in_vmem] * 3,
        out_shape=[
            jax.ShapeDtypeStruct((rows, width), f32),
            jax.ShapeDtypeStruct((nh, keys_here // nh, dim), f32),
            jax.ShapeDtypeStruct((rows, group_heads), f32),
        ],
        scratch_shapes=[
            pltpu.VMEM((heads_here, keys_here, queries), f32),
            pltpu.VMEM((keys_here, queries), f32),
            pltpu.VMEM((keys_here, queries), f32),
            pltpu.VMEM((keys_here, queries), f32),
            pltpu.VMEM((lat, queries), bf16),
            pltpu.VMEM((lat, queries), bf16),
            pltpu.VMEM((2, 2, lat, queries), bf16),
            pltpu.VMEM((2, heads_here, queries), f32),
            pltpu.VMEM((nk - 1, 2, heads_here, queries), f32),
            pltpu.VMEM((heads_here, queries), f32),
            pltpu.VMEM((rows, keys_here), f32),
            pltpu.VMEM((rows, 128), f32),
            pltpu.VMEM((nk - 1, rows, 128), f32),
            pltpu.VMEM((halves, nh, rows, keys_here // halves), f32),
            pltpu.VMEM((nh - 1, halves, rows, keys_here // halves), f32),
            pltpu.VMEM((rows, keys_here), f32),
            pltpu.VMEM((dim, keys_here), f32),
            pltpu.VMEM((nh, keys_here // nh, dim), f32),
            pltpu.VMEM((nh - 1, keys_here // nh, dim), f32),
            pltpu.VMEM((nk, rows, width + 128), f32),
            pltpu.VMEM((nk - 1, rows, width + 128), f32),
            dma(4),
            dma(nk - 1), dma(nk - 1), dma(nk - 1), dma(nk - 1),
            dma(nh - 1, halves), dma(nh - 1, halves),
            dma(nk - 1), dma(nk - 1),
            dma(nh - 1), dma(nh - 1), dma(nh - 1), dma(nh - 1),
        ],
        compiler_params=pltpu.CompilerParams(
            collective_id=0, has_side_effects=True, vmem_limit_bytes=VMEM_LIMIT),
    )(q_latent.transpose(0, 2, 1), k_latent, key_start[None, :], query_pos[None, :], q_index, k_index,
      weights, own_start, own_pos, loss_weight[:, None])
    return (grad_query, grad_key.reshape(keys_here, dim), grad_weight)


def solution(mesh):
    return jax.shard_map(
        shards,
        mesh=mesh,
        in_specs=(
            P("head", None, None),
            P("key", None),
            P("head", None),
            P("key", None),
            P("head", None),
            P("head"),
            P(),
            P(),
        ),
        out_specs=(P("head", "key"), P("key", None), P("head", "key")),
        check_vma=False,
    )
```

time: 343 us -> 103 us (0.30)
  matrix products: 165 us -> 0 us
  Pallas kernels: 0 us -> 87.6 us
  blocking collectives: 57.5 us -> 0 us
  other arithmetic: 46.5 us -> 0 us
  waiting for transfers between devices: 43.3 us -> 0 us
  between operations: 15.2 us -> 0.65 us
    dot_general x67 -> x0, matrix products: 165 us -> none  [the longest x64 142 us: main_scores(): jnp.einsum('qd,sd->qs', q_rows, k_latent, preferred_element_type=jnp.floa...]
    pallas_call x0 -> x1, Pallas kernels: none -> 87.6 us  [shards(): pl.pallas_call(kernel, in_specs=[pl.BlockSpec(memory_space=pl.ANY)] + [in...]
    reduce_sum x34 -> x0, other arithmetic: 44.1 us -> none  [the longest x33 36.5 us: local_stats(): return (highest, jnp.sum(exponents, axis=-1))]
    reduce_scatter x2 -> x0, waiting for transfers between devices: 43.2 us -> none  [the longest x1 39.3 us: shards(): lax.psum_scatter(query_part, 'key', scatter_dimension=1, tiled=True)]
    unnamed x2 -> x0, blocking collectives: 37.5 us -> none
    all_gather x2 -> x0, blocking collectives: 20 us -> none  [joined(): everything = jax.tree.map(lambda part: lax.all_gather(part, axis), x)]
    broadcast_in_dim x0 -> x4, local copies, waits for them, and re-layouts: none -> 3.54 us  [the longest x2 1.48 us: shards(): own_pos = lax.dynamic_slice_in_dim(query_pos, row_start, rows)[:, None]]
    unnamed x24 -> x5, local copies, waits for them, and re-layouts: 6.81 us -> 8.2 us
  transfers between devices with their start and end apart: 3 -> 0, of which waited for: 2 -> 0; matrix products, arithmetic and copies ran while one was open for 8% -> 0% of each run, Pallas kernels for 0% -> 0%
where the time goes in v2:
time: 103 us; the launch traced here: 101 us
  Pallas kernels  87.6 us (85%)
  local copies, waits for them, and re-layouts  12.6 us (12%)
    pallas_call x1, Pallas kernels, shards(): pl.pallas_call(kernel, in_specs=[pl.BlockSpec(memory_space=pl.ANY)] + [in...  87.6 us
    unnamed x5, local copies, waits for them, and re-layouts  8.2 us

profile of v2, /device:TPU:0, one launch (start us, length us, event | category | flops | bytes accessed | tf_op | source)
XLA Modules:
  0.0 100.9 jit_solution(3730865120762589328)
XLA Ops:
  0.6 0.8 dynamic-slice_bitcast_fusion
  1.4 0.7 copy.20.pos_col
  2.1 0.7 copy.19.start_col
  2.8 0.8 copy.16
  3.7 1.4 %copy.21.loss_ref = f32[64,1]{1,0:T(8,128)} copy(f32[64,1]{0,1:T(1,128)} %bitcast.17) | data formatting | bytes 512 | tf_op jit(solution)/shard_map/broadcast_in_dim | solution.py:325
  5.0 0.8 copy.17
  5.8 2.4 %copy.18.k_ref = bf16[1024,576]{1,0:T(8,128)(2,1)} copy(bf16[1024,576]{0,1:T(8,128)(2,1)} %param.9) | data formatting | bytes 2359296 | tf_op args[1]
  8.3 87.6 %shard_map.103 = (f32[64,1024]{1,0:T(8,128)}, f32[4,256,128]{2,1,0:T(8,128)}, f32[64,8]{1,0:T(8,128)}) custom-call(bf16[32,576,256]{2,1,0:T(8,128)(2,1)} %bitcast.11, bf16[1024,576]{1,0:T(8,128)(2,1)} %copy.18.k_ref, s32[1,256]{1,0:T(1,128)} %bitcast.15, s32[1,256]{1,0:T(1,128)} %bitcast.16, bf16[64,8192]{1,0:T(8,128)(2,1)} %qi_ref.1, ...), custom_call_target="tpu_custom_call" | custom-call | tf_op jit(solution)/shard_map/pallas_call | solution.py:285
  95.9 1.4 %copy.22 = f32[64,8]{0,1:T(8,128)} copy(f32[64,8]{1,0:T(8,128)} %get-tuple-element.14) | data formatting | bytes 4096
  97.3 1.7 %copy.25 = f32[64,1024]{1,0:T(8,128)} copy(f32[64,1024]{1,0:T(8,128)} %get-tuple-element.20) | data formatting | bytes 524288
  99.0 1.9 %copy.26 = f32[1024,128]{1,0:T(8,128)} copy(f32[1024,128]{1,0:T(8,128)} %bitcast.13) | data formatting | bytes 1048576

commit v3 on v2

--- a/solution.py
+++ b/solution.py
@@ -22,9 +22,15 @@
     return jnp.concatenate([block[:, i * dim : (i + 1) * dim] for i in range(heads)], axis=0)
 
 
-def kernel(q_hbm, k_ref, start_row, pos_row, qi_ref, ki_ref, w_ref, start_col, pos_col, loss_ref,
+def column(row, first, rows):
+    shape = (rows, row.shape[1])
+    down, across = (lax.broadcasted_iota(jnp.int32, shape, i) for i in (0, 1))
+    return jnp.sum(jnp.where(across == down + first, row, 0.0), axis=1, keepdims=True)
+
+
+def kernel(q_hbm, kt_ref, start_row, pos_row, qi_ref, ki_ref, weight_ref, loss_row,
            gq_ref, gk_ref, gw_ref,
-           e, bias, raw_a, raw_b, q_first, q_last, q_pair, stats, stats_in, coef,
+           k_ref, w_ref, e, bias, raw_a, raw_b, q_first, q_last, q_pair, stats, stats_in, coef,
            iscores, istats, istats_in, t_send, t_in, grads, key_t, key_sum, key_in,
            part_send, part_in,
            q_sem, st_send, st_recv, is_send, is_recv, tg_send, tg_recv, pt_send, pt_recv,
@@ -67,6 +73,9 @@
             pl.semaphore_signal(barrier, inc=1, device_id={axis: peer(axis, offset)},
                                 device_id_type=pl.DeviceIdType.MESH)
 
+    k_ref[...] = kt_ref[...].T
+    for g in range(groups):
+        w_ref[g] = weight_ref[:, g * group_heads : (g + 1) * group_heads]
     position = lax.broadcasted_iota(jnp.int32, bias.shape, 0) + first_key
     bias[...] = jnp.where((position >= start_row[...]) & (position <= pos_row[...]), 0.0, LOW)
 
@@ -131,7 +140,11 @@
 
     lax.fori_loop(0, groups, index_lap, 0)
     position = lax.broadcasted_iota(jnp.int32, (rows, keys_here), 1) + first_key
-    seen = (position >= start_col[...]) & (position <= pos_col[...])
+    own_start = column(start_row[...].astype(f32), my_head * rows, rows)
+    own_pos = column(pos_row[...].astype(f32), my_head * rows, rows)
+    loss = column(loss_row[...], 0, rows)
+    position = position.astype(f32)
+    seen = (position >= own_start) & (position <= own_pos)
     scores = jnp.where(seen, iscores[...] * index_scale, LOW)
     iscores[...] = scores
     high = jnp.maximum(jnp.max(scores, axis=1, keepdims=True), FLOOR)
@@ -195,7 +208,7 @@
         for d in range(1, head_devices):
             target = target + t_in[d - 1, part]
         grads[:, span] = jnp.where(
-            seen[:, span], loss_ref[...] * (iscores[:, span] - target * (1.0 / H)), 0.0)
+            seen[:, span], loss * (iscores[:, span] - target * (1.0 / H)), 0.0)
 
     key_t[...] = jnp.zeros_like(key_t)
 
@@ -275,16 +288,12 @@
     group_heads = index_heads // nk
     width = index_width // nk
     f32, bf16 = jnp.float32, jnp.bfloat16
-    row_start = lax.axis_index("head") * rows
-    own_pos = lax.dynamic_slice_in_dim(query_pos, row_start, rows)[:, None]
-    own_start = lax.dynamic_slice_in_dim(key_start, row_start, rows)[:, None]
-    weights = head_weight.reshape(rows, nk, group_heads).transpose(1, 0, 2)
-    halves = 2
+    halves = 4
     dma = lambda *shape: pltpu.SemaphoreType.DMA(shape)
     in_vmem = pl.BlockSpec(memory_space=pltpu.VMEM)
     grad_query, grad_key, grad_weight = pl.pallas_call(
         kernel,
-        in_specs=[pl.BlockSpec(memory_space=pl.ANY)] + [in_vmem] * 9,
+        in_specs=[pl.BlockSpec(memory_space=pl.ANY)] + [in_vmem] * 7,
         out_specs=[in_vmem] * 3,
         out_shape=[
             jax.ShapeDtypeStruct((rows, width), f32),
@@ -292,6 +301,8 @@
             jax.ShapeDtypeStruct((rows, group_heads), f32),
         ],
         scratch_shapes=[
+            pltpu.VMEM((keys_here, lat), bf16),
+            pltpu.VMEM((nk, rows, group_heads), f32),
             pltpu.VMEM((heads_here, keys_here, queries), f32),
             pltpu.VMEM((keys_here, queries), f32),
             pltpu.VMEM((keys_here, queries), f32),
@@ -321,8 +332,8 @@
         ],
         compiler_params=pltpu.CompilerParams(
             collective_id=0, has_side_effects=True, vmem_limit_bytes=VMEM_LIMIT),
-    )(q_latent.transpose(0, 2, 1), k_latent, key_start[None, :], query_pos[None, :], q_index, k_index,
-      weights, own_start, own_pos, loss_weight[:, None])
+    )(q_latent.transpose(0, 2, 1), k_latent.T, key_start[None, :], query_pos[None, :], q_index, k_index,
+      head_weight, loss_weight[None, :])
     return (grad_query, grad_key.reshape(keys_here, dim), grad_weight)
 
 

time: 103 us -> 94.3 us (0.916); the launches traced: 101 us -> 93.4 us
  local copies, waits for them, and re-layouts: 12.6 us -> 4.96 us
    broadcast_in_dim x4 -> x0, local copies, waits for them, and re-layouts: 3.54 us -> none  [the longest x2 1.48 us: shards(): own_pos = lax.dynamic_slice_in_dim(query_pos, row_start, rows)[:, None]]
    unnamed x5 -> x3, local copies, waits for them, and re-layouts: 8.2 us -> 4.96 us
where the time goes in v3:
time: 94.3 us; the launch traced here: 93.4 us
  Pallas kernels  87.8 us (93%)
  local copies, waits for them, and re-layouts  4.96 us (5%)
    pallas_call x1, Pallas kernels, shards(): pl.pallas_call(kernel, in_specs=[pl.BlockSpec(memory_space=pl.ANY)] + [in...  87.8 us
    unnamed x3, local copies, waits for them, and re-layouts  4.96 us

profile of v3, /device:TPU:0, one launch (start us, length us, event | category | flops | bytes accessed | tf_op | source)
XLA Modules:
  0.0 93.4 jit_solution(14473242465143920063)
XLA Ops:
  0.6 87.8 %shard_map.103 = (f32[64,1024]{1,0:T(8,128)}, f32[4,256,128]{2,1,0:T(8,128)}, f32[64,8]{1,0:T(8,128)}) custom-call(bf16[32,576,256]{2,1,0:T(8,128)(2,1)} %bitcast.6, bf16[576,1024]{1,0:T(8,128)(2,1)} %bitcast.7, s32[1,256]{1,0:T(1,128)} %bitcast.9, s32[1,256]{1,0:T(1,128)} %bitcast.10, bf16[64,8192]{1,0:T(8,128)(2,1)} %qi_ref.1, bf16[1024,128]{1,0:T(8,128)(2,1)} %ki_ref.1, ...), custom_call_target="tpu_custom_call" | custom-call | tf_op jit(solution)/shard_map/pallas_call | solution.py:294
  88.4 1.4 %copy.11 = f32[64,8]{0,1:T(8,128)} copy(f32[64,8]{1,0:T(8,128)} %get-tuple-element.11) | data formatting | bytes 4096
  89.9 1.7 %copy.14 = f32[64,1024]{1,0:T(8,128)} copy(f32[64,1024]{1,0:T(8,128)} %get-tuple-element.15) | data formatting | bytes 524288
  91.5 1.9 %copy.15 = f32[1024,128]{1,0:T(8,128)} copy(f32[1024,128]{1,0:T(8,128)} %bitcast.8) | data formatting | bytes 1048576
